TPU v7x, 256 devices: a whole 4x4x8 slice. The times are simulated.
256 devices in a mesh: row: 16 (over y, z_hi, core), col: 16 (over x, z_lo).
Axes of the slice: x: 4, y: 4, z: 8 (z_hi: 2, z_lo: 4; z = z_hi * 4 + z_lo), core: 2. Of those that a mesh axis runs over, the one named last changes fastest.
Arguments:
- image: float32 [12288, 1280], P(('row', 'col')), may hold values from -1 to 1
- text: float32 [12288, 1280], P(('col', 'row')), may hold values from -1 to 1
- log_scale: float32 [1], replicated, may hold values from 2 to 3
Outputs:
- loss: float32 [1], replicated
- image_grad: float32 [12288, 1280], P(('row', 'col'))
- text_grad: float32 [12288, 1280], P(('col', 'row'))
- scale_grad: float32 [1], replicated
All inputs are finite; a program needn't handle non-finite values.
Results may differ from a plain program's by a relative error of at most 0.0003.
Values sent between devices are 32-bit elements; how exact they have to be, the bound alone decides.
A program may use at most 64 MiB of HBM per device.

v0:
```python
import jax
import jax.numpy as jnp
from jax import lax
from jax.sharding import PartitionSpec as P


def per_device(image, text, log_scale):
    logit_scale = jnp.exp(log_scale[0])
    rows_here = image.shape[0]
    image_block = lax.all_gather(image, "col", axis=0, tiled=True)
    text_block = lax.all_gather(text, "row", axis=0, tiled=True)
    logits = logit_scale * jnp.dot(
        image_block,
        text_block.T,
        precision=lax.Precision.HIGHEST,
        preferred_element_type=jnp.float32,
    )
    row_local = jnp.max(logits, axis=1)
    col_local = jnp.max(logits, axis=0)
    row_peak = lax.pmax(row_local, "col")
    col_peak = lax.pmax(col_local, "row")
    row_total = lax.psum(jnp.sum(jnp.exp(logits - row_peak[:, None]), axis=1), "col")
    col_total = lax.psum(jnp.sum(jnp.exp(logits - col_peak[None, :]), axis=0), "row")
    row_lse = row_peak + jnp.log(row_total)
    col_lse = col_peak + jnp.log(col_total)
    row_index = lax.axis_index("row")
    col_index = lax.axis_index("col")
    tile_rows = logits.shape[0]
    tile_cols = logits.shape[1]
    batch_size = tile_rows * lax.axis_size("row")
    row_ids = row_index * tile_rows + jnp.arange(tile_rows, dtype=jnp.int32)
    col_ids = col_index * tile_cols + jnp.arange(tile_cols, dtype=jnp.int32)
    matching = (row_ids[:, None] == col_ids[None, :]).astype(jnp.float32)
    row_part = jnp.sum(lax.dynamic_slice_in_dim(row_lse, col_index * rows_here, rows_here, 0))
    col_part = jnp.sum(
        lax.dynamic_slice_in_dim(col_lse, row_index * text.shape[0], text.shape[0], 0)
    )
    diagonal = jnp.sum(logits * matching)
    loss_term = (row_part + col_part - 2.0 * diagonal) / (2.0 * batch_size)
    loss_value = lax.psum(loss_term, ("row", "col"))
    weights = (
        0.5 * (jnp.exp(logits - row_lse[:, None]) + jnp.exp(logits - col_lse[None, :])) - matching
    )
    scale_term = jnp.sum(weights * logits) / batch_size
    scale_value = lax.psum(scale_term, ("row", "col"))
    piece = weights
    image_grad = lax.psum_scatter(
        logit_scale
        * jnp.dot(
            piece, text_block, precision=lax.Precision.HIGHEST, preferred_element_type=jnp.float32
        ),
        "col",
        scatter_dimension=0,
        tiled=True,
    )
    piece = weights
    text_grad = lax.psum_scatter(
        logit_scale
        * lax.dot_general(
            piece,
            image_block,
            (((0,), (0,)), ((), ())),
            precision=lax.Precision.HIGHEST,
            preferred_element_type=jnp.float32,
        ),
        "row",
        scatter_dimension=0,
        tiled=True,
    )
    return (loss_value.reshape(1), image_grad, text_grad, scale_value.reshape(1))


def solution(mesh):
    placed = (P(("row", "col"), None), P(("col", "row"), None), P())
    return jax.shard_map(
        per_device,
        mesh=mesh,
        in_specs=placed,
        out_specs=(P(), P(("row", "col"), None), P(("col", "row"), None), P()),
        check_vma=False,
    )
```

profile of v0, /device:TPU:1, one launch (start us, length us, event | category | flops | bytes accessed | tf_op | source)
XLA Modules:
  0.0 574.6 jit_solution(12188416064364384549)
XLA Ops:
  7.2 0.0 all-gather.3.cloned.1.call-start
  7.2 0.7 all-gather.3.cloned.1.call-update
  7.9 0.0 all-gather.5.cloned.1.call-start
  7.9 0.7 all-gather.5.cloned.1.call-update
  8.6 0.0 reduce-scatter.5.cloned.1.call-start
  9.4 97.6 %all-gather.3.cloned.1.call-done = f32[768,1280]{1,0:T(8,128)} async-done(((f32[48,1280]{1,0:T(8,128)}), f32[768,1280]{1,0:T(8,128)}) %all-gather.3.cloned.1.call-update) | async-done | bytes 3932176 | tf_op jit(solution)/shard_map/all_gather | solution.py:10
  107.0 81.1 %all-gather.5.cloned.1.call-done = f32[768,1280]{1,0:T(8,128)} async-done(((f32[48,1280]{1,0:T(8,128)}), f32[768,1280]{1,0:T(8,128)}) %all-gather.5.cloned.1.call-update) | async-done | bytes 3932176 | tf_op jit(solution)/shard_map/all_gather | solution.py:11
  188.1 13.6 %fusion.16 = (f32[768]{0:T(1024)S(1)}, f32[768]{0:T(1024)S(1)}, f32[768,768]{1,0:T(8,128)S(1)}) fusion(f32[768,1280]{1,0:T(8,128)} %all-gather.3.cloned.1.call-done, f32[768,1280]{1,0:T(8,128)} %all-gather.5.cloned.1.call-done, f32[]{:T(128)} %bitcast), kind=kOutput, calls=%fused_computation.28 | convolution fusion | flops 9061464064 | bytes 10229764 | tf_op jit(solution)/shard_map/dot_general | solution.py:12
  201.7 42.4 %pmax.15 = f32[768]{0:T(1024)S(1)} all-reduce(f32[768]{0:T(1024)S(1)} %get-tuple-element.8), channel_id=1, replica_groups=mesh['row'=16,'col'=16] {'row'}, use_global_device_ids=true, to_apply=%region_6.0 | all-reduce | flops 768 | bytes 6144 | tf_op jit(solution)/shard_map/pmax | solution.py:21
  244.1 32.4 %pmax.14 = f32[768]{0:T(1024)S(1)} all-reduce(f32[768]{0:T(1024)S(1)} %get-tuple-element.9), channel_id=1, replica_groups=mesh['row'=16,'col'=16] {'col'}, use_global_device_ids=true, to_apply=%region_1.0 | all-reduce | flops 768 | bytes 6144 | tf_op jit(solution)/shard_map/pmax | solution.py:20
  276.5 1.0 exponential_reduce_fusion
  277.5 52.5 %psum.29 = f32[768]{0:T(1024)S(1)} all-reduce(f32[768]{0:T(1024)S(1)} %get-tuple-element.6), channel_id=1, replica_groups=mesh['row'=16,'col'=16] {'row'}, use_global_device_ids=true, to_apply=%region_8.0 | all-reduce | flops 768 | bytes 6144 | tf_op jit(solution)/shard_map/psum | solution.py:23
  330.1 31.2 %psum.28 = f32[768]{0:T(1024)S(1)} all-reduce(f32[768]{0:T(1024)S(1)} %get-tuple-element.7), channel_id=1, replica_groups=mesh['row'=16,'col'=16] {'col'}, use_global_device_ids=true, to_apply=%region_3.0 | all-reduce | flops 768 | bytes 6144 | tf_op jit(solution)/shard_map/psum | solution.py:22
  361.3 14.3 %convolution_multiply_fusion = f32[768,1280]{1,0:T(8,128)} fusion(f32[768,1280]{1,0:T(8,128)} %all-gather.3.cloned.1.call-done, f32[]{:T(128)} %bitcast, f32[768,768]{1,0:T(8,128)S(1)} %get-tuple-element.12, f32[768]{0:T(1024)S(1)} %log_add_fusion, f32[768]{0:T(1024)S(1)} %log_add_fusion.1, s32[768]{0:T(1024)S(1)} %get-tuple-element.13, ...), kind=kOutput, calls=%fused_computation | convolution fusion | flops 9064808448 | bytes 10235908 | tf_op jit(solution)/shard_map/dot_general | solution.py:59
  375.6 0.0 reduce-scatter.5.cloned.1.call-update
  375.6 0.3 reduce-scatter.3.cloned.1.call-start
  375.9 14.3 %convolution_multiply_fusion.1 = f32[768,1280]{1,0:T(8,128)} fusion(f32[768,1280]{1,0:T(8,128)} %all-gather.5.cloned.1.call-done, f32[]{:T(128)} %bitcast, f32[768,768]{1,0:T(8,128)S(1)} %get-tuple-element.12, f32[768]{0:T(1024)S(1)} %log_add_fusion, f32[768]{0:T(1024)S(1)} %log_add_fusion.1, s32[768]{0:T(1024)S(1)} %get-tuple-element.13, ...), kind=kOutput, calls=%fused_computation.1 | convolution fusion | flops 9064808448 | bytes 10235908 | tf_op jit(solution)/shard_map/dot_general | solution.py:49
  390.2 0.0 reduce-scatter.3.cloned.1.call-update
  390.2 0.7 dynamic-slice_reduce_fusion
  390.9 0.7 dynamic-slice_reduce_fusion.1
  392.9 2.5 multiply_reduce_fusion
  396.7 88.4 %all-reduce = (f32[1]{0:T(128)}, f32[1]{0:T(128)}) all-reduce(f32[1]{0:T(128)} %bitcast.1, f32[1]{0:T(128)} %bitcast.2), channel_id=1, replica_groups=mesh['row'=16,'col'=16] {'row','col'}, use_global_device_ids=true, to_apply=%region_11.0 | all-reduce | flops 2 | bytes 16 | tf_op jit(solution)/shard_map/psum | solution.py:40
  485.1 0.0 reduce-scatter.5.cloned.1.call-done
  485.1 83.0 %reduce-scatter.3.cloned.1.call-done = f32[48,1280]{1,0:T(8,128)} async-done(((f32[768,1280]{1,0:T(8,128)}), f32[48,1280]{1,0:T(8,128)}) %reduce-scatter.3.cloned.1.call-update) | async-done | bytes 245776 | tf_op jit(solution)/shard_map/reduce_scatter | solution.py:47
  (3 shorter events, 0.0 us)
Async XLA Ops:
  7.2 99.8 %all-gather.3.cloned.1.call-start = ((), (), s32[]{:S(2)}) async-start(), calls=%async_computation.2 | async-start | bytes 4177920 | tf_op jit(solution)/shard_map/all_gather | solution.py:10
  7.9 180.2 %all-gather.5.cloned.1.call-start = ((), (), s32[]{:S(2)}) async-start(), calls=%async_computation.3 | async-start | bytes 4177920 | tf_op jit(solution)/shard_map/all_gather | solution.py:11
  8.6 476.5 %reduce-scatter.5.cloned.1.call-start = ((), (), s32[]{:S(2)}) async-start(), calls=%async_computation.5 | async-start | bytes 4177920 | tf_op jit(solution)/shard_map/reduce_scatter | solution.py:57
  375.6 192.5 %reduce-scatter.3.cloned.1.call-start = ((), (), s32[]{:S(2)}) async-start(), calls=%async_computation.4 | async-start | bytes 4177920 | tf_op jit(solution)/shard_map/reduce_scatter | solution.py:47
Sparse Core Ops, SparseCore 0:
  9.8 97.1 all-gather.2
  109.7 78.3 all-gather.4
  375.7 100.2 reduce-scatter.4
  479.1 88.9 reduce-scatter.2
where the time goes:
time: 584 us; the launch traced here: 575 us
  waiting for transfers between devices  263 us (45%)
  blocking collectives  247 us (42%)
  matrix products  42.2 us (7%)
  between operations  17.1 us (3%)
    all_gather x1, waiting for transfers between devices, per_device(): image_block = lax.all_gather(image, 'col', axis=0, tiled=True)  97.6 us
    psum x1, blocking collectives, per_device(): loss_value = lax.psum(loss_term, ('row', 'col'))  88.4 us
    reduce_scatter x1, waiting for transfers between devices, per_device(): lax.psum_scatter(logit_scale * jnp.dot(piece, text_block, precision=lax.P...  83 us
    all_gather x1, waiting for transfers between devices, per_device(): text_block = lax.all_gather(text, 'row', axis=0, tiled=True)  81.1 us
    psum x1, blocking collectives, per_device(): lax.psum(jnp.sum(jnp.exp(logits - col_peak[None, :]), axis=0), 'row')  52.5 us
    pmax x1, blocking collectives, per_device(): col_peak = lax.pmax(col_local, 'row')  42.4 us
    pmax x1, blocking collectives, per_device(): row_peak = lax.pmax(row_local, 'col')  32.4 us
    psum x1, blocking collectives, per_device(): lax.psum(jnp.sum(jnp.exp(logits - row_peak[:, None]), axis=1), 'col')  31.2 us
  transfers between devices with their start and end apart: 4, of which 3 were waited for; matrix products, arithmetic and copies ran while one was open for 3% of the time, Pallas kernels for 0%

commit v1 on v0

v1 whole, which is shorter than its diff:
```python
import functools

import jax
import jax.numpy as jnp
from jax import lax
from jax.experimental import pallas as pl
from jax.experimental.pallas import tpu as pltpu
from jax.sharding import PartitionSpec as P

MESH = pl.DeviceIdType.MESH
F32 = jnp.float32
BF16 = jnp.bfloat16

NX, NZ = 4, 8
IMG = [(0, 0), (3, 0), (1, 0), (0, 3), (0, 1),
       (3, 3), (3, 1), (1, 3), (1, 1), (0, 2), (2, 0),
       (3, 2), (2, 3), (1, 2), (2, 1), (2, 2)]
TXT = [(dz, dk) for dz in (0, 7, 1, 6, 2, 5, 3, 4) for dk in (0, 1)]
ISLOT = {p: i for i, p in enumerate(IMG)}
TSLOT = {p: i for i, p in enumerate(TXT)}
PLANE = [(x, y, 0, 0) for x in (2, 3, 1, 0) for y in (2, 3, 1, 0) if (x, y) != (0, 0)]
RING = [(0, 0, z, k) for z in (4, 3, 5, 2, 6, 1, 7, 0) for k in (1, 0) if (z, k) != (0, 0)]
N_COPIES = 192
LN2 = 0.6931471805599453


def position():
    r, c = lax.axis_index("row"), lax.axis_index("col")
    return c // 4, r // 4, ((r // 2) % 2) * 4 + c % 4, r % 2


def shard_of(image, x, y, z, k):
    row, col = (y * 2 + z // 4) * 2 + k, x * 4 + z % 4
    return row * 16 + col if image else col * 16 + row


def split(v):
    hi = v.astype(BF16)
    return hi, (v - hi.astype(F32)).astype(BF16)


def dot3(ah, al, bh, bl, dims):
    d = functools.partial(lax.dot_general, dimension_numbers=(dims, ((), ())), preferred_element_type=F32)
    return d(ah, bh) + (d(al, bh) + d(ah, bl))


def kernel(R, E, batch, im, tx, ls, out_i, out_t, out_loss, out_scale,
           img, txt, ih, il, th, tl, lg, wh, wl, wth, wtl, gi, gt,
           rq, ru, rpq, rpu, rz, rc, cols_a, cols_b, rst, cst, pst, zst, rid, ssem, rsem):
    H = R // 2
    EH = E // 2
    N = 16 * R
    x, y, z, k = position()

    def peer(o):
        px, py, pz, pk = (x + o[0]) % 4, (y + o[1]) % 4, (z + o[2]) % 8, (k + o[3]) % 2
        return ((py * 2 + pz // 4) * 2 + pk, px * 4 + pz % 4)

    copies = []

    def send(src, dst, o):
        i = len(copies)
        c = pltpu.make_async_remote_copy(src_ref=src, dst_ref=dst, send_sem=ssem.at[i], recv_sem=rsem.at[i],
                                         device_id=peer(o), device_id_type=MESH)
        c.start()
        copies.append(c)
        return c

    CORE = (0, 0, 0, 1)

    def zdir(s):
        return (0, 0, s % 8, 0)

    def idir(h, primary, s):
        return (s % 4, 0, 0, 0) if (h == 0) == primary else (0, s % 4, 0, 0)

    def pos(h, p, q):
        p, q = p % 4, q % 4
        return (p, q) if h == 0 else (q, p)

    HALF = {"f": pl.ds(0, E), "A": pl.ds(0, EH), "B": pl.ds(EH, EH)}

    barrier = pltpu.get_barrier_semaphore()
    for o in PLANE + RING:
        pl.semaphore_signal(barrier, inc=1, device_id=peer(o), device_id_type=MESH)
    for s, (dx, dy) in enumerate(IMG):
        rid[s] = shard_of(True, (x + dx) % 4, (y + dy) % 4, z, k) * R
    pl.semaphore_wait(barrier, len(PLANE) + len(RING))

    got = {}

    def isend(h, p, q, primary, s, part="f"):
        o = pos(h, p, q)
        rows = pl.ds(h * H, H)
        src = im.at[rows, HALF[part]] if o == (0, 0) else img.at[ISLOT[o], rows, HALF[part]]
        to = pos(h, p - s, q) if primary else pos(h, p, q - s)
        got[("i", h, to, part)] = send(src, img.at[ISLOT[to], rows, HALF[part]], idir(h, primary, s))

    def iwait(h, p, q):
        o = pos(h, p, q)
        for part in ("f", "A", "B"):
            c = got.pop(("i", h, o, part), None)
            if c is not None:
                c.wait_recv()

    def tsend(dz, s, part):
        rows = pl.ds(0 if part == "a" else H, H)
        src = tx.at[rows, :] if dz == 0 else txt.at[TSLOT[(dz, 0)], rows, :]
        to = (dz - s) % 8
        got[("t", to, part)] = send(src, txt.at[TSLOT[(to, 0)], rows, :], zdir(s))

    def twait(dz, part):
        got.pop(("t", dz, part)).wait_recv()

    def tcore(dz):
        src = tx if dz == 0 else txt.at[TSLOT[(dz, 0)]]
        got[("c", dz)] = send(src, txt.at[TSLOT[(dz, 1)]], CORE)

    def cwait(dz):
        got.pop(("c", dz)).wait_recv()

    def put(hi_ref, lo_ref, s, v):
        rows = pl.ds(s * R if isinstance(s, int) else pl.multiple_of(s * R, R), R)
        hi_ref[rows, :], lo_ref[rows, :] = split(v)

    def conv(ref, hi_ref, lo_ref, a, b):
        def body(s, _):
            put(hi_ref, lo_ref, s, ref[s])
            return 0
        lax.fori_loop(a, b, body, 0)

    scale = jnp.exp(jnp.full((1, 1), ls[0], F32))

    def logits(a, b, t0, t1):
        rows = slice(a * R, b * R)

        def body(t, _):
            cs = pl.ds(pl.multiple_of(t * 256, 256), 256)
            lg[rows, cs] = scale * dot3(ih[rows, :], il[rows, :], th[cs, :], tl[cs, :], ((1,), (1,)))
            return 0
        lax.fori_loop(t0, t1, body, 0)

    for primary in (True, False):
        for h in (0, 1):
            isend(h, 0, 0, primary, 1)
            isend(h, 0, 0, primary, -1)
        if primary:
            for part in ("a", "b"):
                tsend(0, 1, part)
                tsend(0, -1, part)
    tcore(0)
    put(ih, il, 0, im[...])
    put(th, tl, 0, tx[...])

    for h in (0, 1):
        iwait(h, 3, 0)
        iwait(h, 1, 0)
        isend(h, 3, 0, True, 1, "A")
        isend(h, 1, 0, True, -1, "B")
    twait(7, "a")
    twait(1, "a")
    tsend(7, 1, "a")
    tsend(1, -1, "a")
    for h in (0, 1):
        for p in (3, 1):
            isend(h, p, 0, False, 1)
            isend(h, p, 0, False, -1)
    cwait(0)
    for h in (0, 1):
        iwait(h, 0, 3)
        iwait(h, 0, 1)
        isend(h, 0, 3, False, 1, "A")
        isend(h, 0, 1, False, -1, "B")
    twait(7, "b")
    twait(1, "b")
    tsend(7, 1, "b")
    tsend(1, -1, "b")
    tcore(7)
    tcore(1)
    conv(img, ih, il, 1, 5)
    for h in (0, 1):
        iwait(h, 2, 0)
        isend(h, 2, 0, False, 1)
        isend(h, 2, 0, False, -1)
    cwait(7)
    cwait(1)
    conv(txt, th, tl, 1, 6)
    twait(6, "a")
    twait(2, "a")
    tsend(6, 1, "a")
    tsend(2, -1, "a")
    logits(0, 5, 0, 1)
    for h in (0, 1):
        for p in (3,):
            iwait(h, p, 3)
            iwait(h, p, 1)
            isend(h, p, 3, False, 1, "A")
            isend(h, p, 1, False, -1, "B")
    twait(6, "b")
    twait(2, "b")
    tsend(6, 1, "b")
    tsend(2, -1, "b")
    tcore(6)
    tcore(2)
    for h in (0, 1):
        for p in (1,):
            iwait(h, p, 3)
            iwait(h, p, 1)
            isend(h, p, 3, False, 1, "A")
            isend(h, p, 1, False, -1, "B")
    twait(5, "a")
    twait(3, "a")
    tsend(5, 1, "a")
    for h in (0, 1):
        iwait(h, 0, 2)
    conv(img, ih, il, 5, 11)
    logits(5, 11, 0, 1)
    cwait(6)
    cwait(2)
    conv(txt, th, tl, 6, 10)
    for h in (0, 1):
        iwait(h, 2, 3)
        iwait(h, 2, 1)
        isend(h, 2, 3, False, 1, "A")
        isend(h, 2, 1, False, -1, "B")
    twait(5, "b")
    twait(3, "b")
    tsend(3, -1, "b")
    tcore(5)
    tcore(3)
    cwait(5)
    cwait(3)
    conv(txt, th, tl, 10, 14)
    logits(0, 11, 1, 2)
    twait(4, "a")
    twait(4, "b")
    tcore(4)
    for h in (0, 1):
        iwait(h, 3, 2)
        iwait(h, 1, 2)
    conv(img, ih, il, 11, 15)
    cwait(4)
    conv(txt, th, tl, 14, 16)
    logits(0, 11, 2, 3)
    for h in (0, 1):
        iwait(h, 2, 2)
    conv(img, ih, il, 15, 16)
    logits(11, 16, 0, 3)

    RB = 2 * R
    NB = N // RB

    def rows_body(i, cm):
        rows = pl.ds(pl.multiple_of(i * RB, RB), RB)
        v = lg[rows, :]
        rm = jnp.max(v, axis=1, keepdims=True)
        rl = rm + jnp.log(jnp.sum(jnp.exp(v - rm), axis=1, keepdims=True))
        cols_a[rows, :] = jnp.broadcast_to(rl, (RB, 128))
        return jnp.maximum(cm, jnp.max(v.reshape(RB // 8, 8, N), axis=0))

    cm = lax.fori_loop(0, NB, rows_body, jnp.full((8, N), -jnp.inf, F32))
    cm = jnp.max(cm, axis=0, keepdims=True)

    def cols_body(i, cs):
        v = lg[pl.ds(pl.multiple_of(i * RB, RB), RB), :]
        return cs + jnp.sum(jnp.exp(v - cm).reshape(RB // 8, 8, N), axis=0)

    cs = lax.fori_loop(0, NB, cols_body, jnp.zeros((8, N), F32))
    cl = cm + jnp.log(jnp.sum(cs, axis=0, keepdims=True))

    NL = N // 128
    lane = lax.broadcasted_iota(jnp.int32, (128, 128), 1)

    def to_rows(ref):
        m = jnp.zeros((128, 128), F32)
        for b in range(NL):
            m = jnp.where(lane == b, ref[b * 128:(b + 1) * 128, :], m)
        return m.T[:8, :]

    def to_cols(ref, v):
        m = jnp.concatenate([v, jnp.zeros((120, 128), F32)], axis=0).T
        for b in range(NL):
            ref[b * 128:(b + 1) * 128, :] = jnp.broadcast_to(m[:, b:b + 1], (128, 128))

    def iabs(s):
        return ((x + IMG[s][0]) % 4) * 4 + (y + IMG[s][1]) % 4

    def tabs(s):
        return ((z + TXT[s][0]) % 8) * 2 + (k + TXT[s][1]) % 2

    def to_abs(where):
        for s in range(16):
            cols_b[pl.ds(pl.multiple_of(where(s) * R, R), R), :] = cols_a[s * R:(s + 1) * R, :]

    def to_rel(where):
        for s in range(16):
            cols_a[s * R:(s + 1) * R, :] = cols_b[pl.ds(pl.multiple_of(where(s) * R, R), R), :]

    me_p, me_r = x * 4 + y, z * 2 + k
    to_abs(iabs)
    rst[me_p] = to_rows(cols_b)
    plane = [send(rst.at[me_p], rst.at[me_p], o) for o in PLANE]
    c8 = jnp.concatenate([cl[:, b * 128:(b + 1) * 128] for b in range(NL)] + [jnp.zeros((8 - NL, 128), F32)], axis=0)
    to_cols(cols_a, c8)
    to_abs(tabs)
    cst[me_r] = to_rows(cols_b)
    ring = [send(cst.at[me_r], cst.at[me_r], o) for o in RING]

    def merge(ref):
        v = ref[...]
        m = jnp.max(v, axis=0)
        return m + jnp.log(jnp.sum(jnp.exp(v - m[None]), axis=0))

    lane_n = lax.broadcasted_iota(jnp.int32, (1, N), 1)
    cid = lane_n
    for s, (dz, dk) in enumerate(TXT):
        base = shard_of(False, x, y, (z + dz) % 8, (k + dk) % 2) * R - s * R
        cid = jnp.where((lane_n >= s * R) & (lane_n < (s + 1) * R), lane_n + base, cid)

    for c in ring:
        c.wait_recv()
    to_cols(cols_b, merge(cst))
    to_rel(tabs)
    c8 = to_rows(cols_a)
    cl = jnp.concatenate([c8[b:b + 1, :] for b in range(NL)], axis=1)
    for c in plane:
        c.wait_recv()
    to_cols(cols_b, merge(rst))
    to_rel(iabs)
    col_sum = jnp.sum(jnp.where(lane_n < R, cl, 0.0))
    row_sum = jnp.sum(cols_a[0:R, 0:1])
    cl2 = cl + LN2

    sub = lax.broadcasted_iota(jnp.int32, (R, N), 0)

    def weights(s):
        rows = pl.ds(pl.multiple_of(s * R, R), R)
        v = lg[rows, :]
        w = jnp.exp(v - (cols_a[rows, 0:1] + LN2)) + jnp.exp(v - cl2)
        hit = (cid - rid[s]) == sub
        return rows, v, hit, jnp.where(hit, w - 1.0, w)

    def weights_body(s, _):
        rows, v, hit, w = weights(s)
        wh[rows, :], wl[rows, :] = split(w)
        return 0

    lax.fori_loop(0, 16, weights_body, 0)

    def transpose(b0, b1):
        def body(b, _):
            cs = pl.ds(pl.multiple_of(b * 128, 128), 128)
            wth[cs, :] = wh[:, cs].T
            wtl[cs, :] = wl[:, cs].T
            return 0
        lax.fori_loop(b0, b1, body, 0)

    def product(dst, ah, al, bh, bl, a, b):
        rows = slice(a * R, b * R)

        def body(n, _):
            cs = pl.ds(pl.multiple_of(n * 256, 256), 256)
            dst[rows, cs] = dot3(ah[rows, :], al[rows, :], bh[:, cs], bl[:, cs], ((1,), (0,)))
            return 0
        lax.fori_loop(0, E // 256, body, 0)

    def image_product(a, b):
        product(gi, wh, wl, th, tl, a, b)

    def text_product(a, b):
        product(gt, wth, wtl, ih, il, a, b)

    COL = {"f": slice(0, E), "A": slice(0, EH), "B": slice(EH, E)}
    red = {}

    def grows(h, o):
        return ISLOT[o] * R + h * H

    def quarter(h, p):
        o = pos(h, p, 2)
        r = pl.ds(grows(h, o), H)
        red[("q", h, p, 1)] = send(gi.at[r, HALF["A"]], rq.at[h, p, 0], idir(h, False, 1))
        red[("q", h, p, 3)] = send(gi.at[r, HALF["B"]], rq.at[h, p, 1], idir(h, False, -1))

    def unit(h, p):
        for q, part, j, s in ((1, "A", 0, 1), (3, "B", 1, -1)):
            red.pop(("q", h, p, q)).wait_recv()
            a = grows(h, pos(h, p, q))
            gi[a:a + H, COL[part]] += rq[h, p, j]
            red[("u", h, p, q)] = send(gi.at[pl.ds(a, H), :], ru.at[h, p, j], idir(h, False, s))

    def gathered(h, p):
        a = grows(h, pos(h, p, 0))
        for q in (1, 3):
            red.pop(("u", h, p, q)).wait_recv()
        gi[a:a + H, :] += ru[h, p, 0] + ru[h, p, 1]

    def pquarter(h):
        r = pl.ds(grows(h, pos(h, 2, 0)), H)
        red[("pq", h, 1)] = send(gi.at[r, HALF["A"]], rpq.at[h, 0], idir(h, True, 1))
        red[("pq", h, 3)] = send(gi.at[r, HALF["B"]], rpq.at[h, 1], idir(h, True, -1))

    def punit(h):
        for p, part, j, s in ((1, "A", 0, 1), (3, "B", 1, -1)):
            red.pop(("pq", h, p)).wait_recv()
            a = grows(h, pos(h, p, 0))
            gi[a:a + H, COL[part]] += rpq[h, j]
            red[("pu", h, p)] = send(gi.at[pl.ds(a, H), :], rpu.at[h, j], idir(h, True, s))

    def image_out(h):
        for p in (1, 3):
            red.pop(("pu", h, p)).wait_recv()
        a = grows(h, (0, 0))
        out_i[h * H:(h + 1) * H, :] = scale * (gi[a:a + H, :] + (rpu[h, 0] + rpu[h, 1]))

    ZR = {"a": 0, "b": H}

    def core_send(dz):
        red[("c", dz)] = send(gt.at[pl.ds(TSLOT[(dz, 1)] * R, R), :], rc.at[dz], CORE)

    def core_add(dz):
        red.pop(("c", dz)).wait_recv()
        a = TSLOT[(dz, 0)] * R
        gt[a:a + R, :] += rc[dz]

    def zsend(dz, s, part):
        a = TSLOT[(dz, 0)] * R + ZR[part]
        to = (dz - s) % 8
        j = 0 if part == "a" else 1
        red[("z", to, s, part)] = send(gt.at[pl.ds(a, H), :], rz.at[dz, j], zdir(s))

    def zadd(dz, s, part):
        red.pop(("z", dz, s, part)).wait_recv()
        a = TSLOT[(dz, 0)] * R + ZR[part]
        j = 0 if part == "a" else 1
        gt[a:a + H, :] += rz[(dz + s) % 8, j]

    transpose(NL // 2, NL)
    text_product(10, 16)
    for dz in (4, 3, 5):
        core_send(dz)
    image_product(11, 16)
    for h in (0, 1):
        quarter(h, 2)
    core_add(4)
    zsend(4, 1, "a")
    zsend(4, -1, "b")
    for p in (3, 1):
        for h in (0, 1):
            quarter(h, p)
    core_add(3)
    core_add(5)
    zsend(3, 1, "b")
    zsend(5, -1, "a")
    image_product(5, 11)
    for h in (0, 1):
        unit(h, 2)
    for h in (0, 1):
        quarter(h, 0)
    transpose(0, NL // 2)
    text_product(6, 10)
    for dz in (2, 6):
        core_send(dz)
    zadd(3, 1, "a")
    zsend(3, 1, "a")
    zadd(5, -1, "b")
    zsend(5, -1, "b")
    for p in (3, 1):
        for h in (0, 1):
            unit(h, p)
    core_add(2)
    core_add(6)
    text_product(0, 6)
    for dz in (1, 7, 0):
        core_send(dz)
    zadd(2, 1, "b")
    zsend(2, 1, "b")
    zadd(6, -1, "a")
    zsend(6, -1, "a")
    image_product(0, 5)
    for h in (0, 1):
        gathered(h, 2)
        pquarter(h)
    zadd(2, 1, "a")
    zsend(2, 1, "a")
    zadd(6, -1, "b")
    zsend(6, -1, "b")
    for dz in (1, 7, 0):
        core_add(dz)
    for h in (0, 1):
        unit(h, 0)

    def sums_body(s, c):
        rows, v, hit, w = weights(s)
        a, d = c
        a = a + jnp.sum((w * v).reshape(R // 8, 8, N), axis=0)
        d = d + jnp.sum(jnp.where(hit, v, 0.0).reshape(R // 8, 8, N), axis=0)
        return a, d

    zero = jnp.zeros((8, N), F32)
    sw, sd = lax.fori_loop(0, 16, sums_body, (zero, zero))
    scale_part = jnp.sum(sw) / batch
    loss_part = (row_sum + col_sum - 2.0 * jnp.sum(sd)) / (2.0 * batch)
    sub8 = lax.broadcasted_iota(jnp.int32, (8, 128), 0)
    pst[me_p] = jnp.where(sub8 == 0, loss_part, jnp.where(sub8 == 1, scale_part, 0.0))
    plane = [send(pst.at[me_p], pst.at[me_p], o) for o in PLANE]

    zadd(1, 1, "b")
    zsend(1, 1, "b")
    zadd(7, -1, "a")
    zsend(7, -1, "a")
    for h in (0, 1):
        gathered(h, 3)
        gathered(h, 1)
        punit(h)
    zadd(1, 1, "a")
    zsend(1, 1, "a")
    zadd(7, -1, "b")
    zsend(7, -1, "b")
    for c in plane:
        c.wait_recv()
    zst[me_r] = jnp.sum(pst[...], axis=0)
    ring = [send(zst.at[me_r], zst.at[me_r], o) for o in RING]
    for h in (0, 1):
        gathered(h, 0)
    zadd(0, 1, "b")
    zadd(0, -1, "a")
    for c in ring:
        c.wait_recv()
    total = jnp.sum(zst[...], axis=0)
    out_loss[0] = jnp.max(total[0:1, 0:1])
    out_scale[0] = jnp.max(total[1:2, 0:1])
    zadd(0, 1, "a")
    zadd(0, -1, "b")
    out_t[...] = scale * gt[0:R, :]
    for h in (0, 1):
        image_out(h)
    for c in copies:
        c.wait_send()


def per_device(image, text, log_scale):
    R, E = image.shape
    N = 16 * R
    batch = 256 * R
    H, EH = R // 2, E // 2
    vm = pltpu.VMEM
    vspec = pl.BlockSpec(memory_space=pltpu.VMEM)
    sspec = pl.BlockSpec(memory_space=pltpu.SMEM)
    one = jax.ShapeDtypeStruct((1,), F32)
    gi, gt, loss, sg = pl.pallas_call(
        functools.partial(kernel, R, E, float(batch)),
        out_shape=(jax.ShapeDtypeStruct((R, E), F32), jax.ShapeDtypeStruct((R, E), F32), one, one),
        in_specs=[vspec, vspec, sspec],
        out_specs=(vspec, vspec, sspec, sspec),
        scratch_shapes=[
            vm((16, R, E), F32), vm((16, R, E), F32),
            vm((N, E), BF16), vm((N, E), BF16), vm((N, E), BF16), vm((N, E), BF16),
            vm((N, N), F32), vm((N, N), BF16), vm((N, N), BF16), vm((N, N), BF16), vm((N, N), BF16),
            vm((N, E), F32), vm((N, E), F32),
            vm((2, 4, 2, H, EH), F32), vm((2, 4, 2, H, E), F32),
            vm((2, 2, H, EH), F32), vm((2, 2, H, E), F32),
            vm((8, 2, H, E), F32), vm((8, R, E), F32),
            vm((N, 128), F32), vm((N, 128), F32),
            vm((16, 8, 128), F32), vm((16, 8, 128), F32), vm((16, 8, 128), F32), vm((16, 8, 128), F32),
            pltpu.SMEM((16,), jnp.int32),
            pltpu.SemaphoreType.DMA((N_COPIES,)), pltpu.SemaphoreType.DMA((N_COPIES,)),
        ],
        compiler_params=pltpu.CompilerParams(collective_id=0, has_side_effects=True, vmem_limit_bytes=60 * 2**20),
        cost_estimate=pl.CostEstimate(flops=18 * N * N * E, bytes_accessed=16 * R * E, transcendentals=6 * N * N),
    )(image, text, log_scale)
    return loss, gi, gt, sg


def solution(mesh):
    return jax.shard_map(
        per_device,
        mesh=mesh,
        in_specs=(P(("row", "col"), None), P(("col", "row"), None), P()),
        out_specs=(P(), P(("row", "col"), None), P(("col", "row"), None), P()),
        check_vma=False,
    )
```

time: 584 us -> 94.2 us (0.16); the launches traced: 575 us -> 94 us
  waiting for transfers between devices: 263 us -> 0 us
  blocking collectives: 247 us -> 0 us
  Pallas kernels: 0 us -> 86.8 us
  matrix products: 42.2 us -> 0 us
  between operations: 17.1 us -> 4.81 us
    all_gather x2 -> x0, waiting for transfers between devices: 179 us -> none  [the longest x1 97.6 us: per_device(): image_block = lax.all_gather(image, 'col', axis=0, tiled=True)]
    psum x3 -> x0, blocking collectives: 172 us -> none  [the longest x1 88.4 us: per_device(): loss_value = lax.psum(loss_term, ('row', 'col'))]
    pallas_call x0 -> x1, Pallas kernels: none -> 86.8 us  [per_device(): pl.pallas_call(functools.partial(kernel, R, E, float(batch)), out_shape=(...]
    reduce_scatter x2 -> x0, waiting for transfers between devices: 83 us -> none  [the longest x1 83 us: per_device(): lax.psum_scatter(logit_scale * jnp.dot(piece, text_block, precision=lax.P...]
    pmax x2 -> x0, blocking collectives: 74.8 us -> none  [the longest x1 42.4 us: per_device(): col_peak = lax.pmax(col_local, 'row')]
    dot_general x3 -> x0, matrix products: 42.2 us -> none  [the longest x1 14.3 us: per_device(): jnp.dot(piece, text_block, precision=lax.Precision.HIGHEST, preferred_ele...]
  transfers between devices with their start and end apart: 4 -> 0, of which waited for: 3 -> 0; matrix products, arithmetic and copies ran while one was open for 3% -> 0% of each run, Pallas kernels for 0% -> 0%
where the time goes in v1:
time: 94.2 us; the launch traced here: 94 us
  Pallas kernels  86.8 us (92%)
  between operations  4.81 us (5%)
  local copies, waits for them, and re-layouts  2.39 us (3%)
    pallas_call x1, Pallas kernels, per_device(): pl.pallas_call(functools.partial(kernel, R, E, float(batch)), out_shape=(...  86.8 us
    unnamed x4, local copies, waits for them, and re-layouts  2.39 us

profile of v1, /device:TPU:1, one launch (start us, length us, event | category | flops | bytes accessed | tf_op | source)
XLA Modules:
  0.0 94.0 jit_solution(11244696697384809982)
XLA Ops:
  1.3 86.8 %shard_map.66 = (f32[48,1280]{1,0:T(8,128)}, f32[48,1280]{1,0:T(8,128)}, f32[1]{0:T(128)}, f32[1]{0:T(128)}) custom-call(f32[48,1280]{1,0:T(8,128)} %im.1, f32[48,1280]{1,0:T(8,128)} %tx.1, f32[1]{0:T(128)S(6)} %copy.11.ls), custom_call_target="tpu_custom_call" | custom-call | flops 13589544960 | bytes 983040 | tf_op jit(solution)/shard_map/pallas_call | solution.py:551
  88.8 0.0 copy-start
  88.8 1.7 %copy.13 = f32[48,1280]{1,0:T(8,128)} copy(f32[48,1280]{1,0:T(8,128)} %get-tuple-element.17) | data formatting | bytes 491520
  90.5 0.0 copy-done
  90.5 0.7 copy.14
Async XLA Ops:
  88.8 1.7 %copy-start = (f32[48,1280]{1,0:T(8,128)S(1)}, f32[48,1280]{1,0:T(8,128)}, u32[]{:S(2)}) copy-start(f32[48,1280]{1,0:T(8,128)} %get-tuple-element.18) | copy-start | bytes 737284

commit v2 on v1

v2 whole, which is shorter than its diff:
```python
import functools

import jax
import jax.numpy as jnp
from jax import lax
from jax.experimental import pallas as pl
from jax.experimental.pallas import tpu as pltpu
from jax.sharding import PartitionSpec as P

MESH = pl.DeviceIdType.MESH
F32 = jnp.float32
BF16 = jnp.bfloat16

NX, NZ = 4, 8
IMG = [(0, 0), (3, 0), (1, 0), (0, 3), (0, 1),
       (3, 3), (3, 1), (1, 3), (1, 1), (0, 2), (2, 0),
       (3, 2), (2, 3), (1, 2), (2, 1), (2, 2)]
TXT = [(dz, dk) for dz in (0, 7, 1, 6, 2, 5, 3, 4) for dk in (0, 1)]
ISLOT = {p: i for i, p in enumerate(IMG)}
TSLOT = {p: i for i, p in enumerate(TXT)}
PLANE = [(x, y, 0, 0) for x in (2, 3, 1, 0) for y in (2, 3, 1, 0) if (x, y) != (0, 0)]
RING = [(0, 0, z, k) for z in (4, 3, 5, 2, 6, 1, 7, 0) for k in (1, 0) if (z, k) != (0, 0)]
N_COPIES = 208
CHUNK = {0: (0, 16), 1: (16, 16), 2: (32, 16), "p": (16, 8), "m": (24, 8)}


def position():
    r, c = lax.axis_index("row"), lax.axis_index("col")
    return c // 4, r // 4, ((r // 2) % 2) * 4 + c % 4, r % 2


def shard_of(image, x, y, z, k):
    row, col = (y * 2 + z // 4) * 2 + k, x * 4 + z % 4
    return row * 16 + col if image else col * 16 + row


def split(v):
    hi = v.astype(BF16)
    return hi, (v - hi.astype(F32)).astype(BF16)


def dot3(ah, al, bh, bl, dims):
    d = functools.partial(lax.dot_general, dimension_numbers=(dims, ((), ())), preferred_element_type=F32)
    return d(ah, bh) + (d(al, bh) + d(ah, bl))


def kernel(R, E, batch, im, tx, ls_hbm, out_i, out_t, out_s,
           img, txt, ih, il, th, tl, lg, er, ec, wh, wl, wth, wtl, gi, gt,
           rq, ru, rpq, rpu, rz, rc, cols_a, cols_b, row_max, row_dot, rst, cst, pst, zst, ls, rid, lsem, ssem, rsem):
    H = R // 2
    EH = E // 2
    N = 16 * R
    x, y, z, k = position()

    def peer(o):
        px, py, pz, pk = (x + o[0]) % 4, (y + o[1]) % 4, (z + o[2]) % 8, (k + o[3]) % 2
        return ((py * 2 + pz // 4) * 2 + pk, px * 4 + pz % 4)

    copies = []

    def send(src, dst, o):
        i = len(copies)
        c = pltpu.make_async_remote_copy(src_ref=src, dst_ref=dst, send_sem=ssem.at[i], recv_sem=rsem.at[i],
                                         device_id=peer(o), device_id_type=MESH)
        c.start()
        copies.append(c)
        return c

    CORE = (0, 0, 0, 1)

    def zdir(s):
        return (0, 0, s % 8, 0)

    def idir(h, primary, s):
        return (s % 4, 0, 0, 0) if (h == 0) == primary else (0, s % 4, 0, 0)

    def pos(h, p, q):
        p, q = p % 4, q % 4
        return (p, q) if h == 0 else (q, p)

    HALF = {"f": pl.ds(0, E), "A": pl.ds(0, EH), "B": pl.ds(EH, EH)}

    barrier = pltpu.get_barrier_semaphore()
    for o in PLANE + RING:
        pl.semaphore_signal(barrier, inc=1, device_id=peer(o), device_id_type=MESH)
    local = [pltpu.make_async_copy(im, img.at[0], lsem.at[0]), pltpu.make_async_copy(tx, txt.at[0], lsem.at[1]),
             pltpu.make_async_copy(ls_hbm, ls, lsem.at[2])]
    for c in local:
        c.start()
    for s, (dx, dy) in enumerate(IMG):
        rid[s] = shard_of(True, (x + dx) % 4, (y + dy) % 4, z, k) * R
    for c in local:
        c.wait()
    pl.semaphore_wait(barrier, len(PLANE) + len(RING))

    got = {}

    def isend(h, p, q, primary, s, part="f"):
        o = pos(h, p, q)
        rows = pl.ds(h * H, H)
        src = img.at[ISLOT[o], rows, HALF[part]]
        to = pos(h, p - s, q) if primary else pos(h, p, q - s)
        got[("i", h, to, part)] = send(src, img.at[ISLOT[to], rows, HALF[part]], idir(h, primary, s))

    def iwait(h, p, q):
        o = pos(h, p, q)
        for part in ("f", "A", "B"):
            c = got.pop(("i", h, o, part), None)
            if c is not None:
                c.wait_recv()

    def tsend(dz, s, ch):
        rows = pl.ds(*CHUNK[ch])
        to = (dz - s) % 8
        got[("t", to, ch)] = send(txt.at[TSLOT[(dz, 0)], rows, :], txt.at[TSLOT[(to, 0)], rows, :], zdir(s))

    def tpass(d, ch):
        for dz, s in ((8 - d, 1), (d, -1)):
            got.pop(("t", dz, ch)).wait_recv()
            nxt = ch if d < 3 else {(1, 0): 0, (1, 1): "p", (-1, 1): "m", (-1, 2): 2}.get((s, ch))
            if nxt is not None:
                tsend(dz, s, nxt)

    def tlast():
        for ch in (0, "p", "m", 2):
            got.pop(("t", 4, ch)).wait_recv()

    def tcore(dz):
        got[("c", dz)] = send(txt.at[TSLOT[(dz, 0)]], txt.at[TSLOT[(dz, 1)]], CORE)

    def cwait(dz):
        got.pop(("c", dz)).wait_recv()

    def put(hi_ref, lo_ref, s, v):
        rows = pl.ds(s * R if isinstance(s, int) else pl.multiple_of(s * R, R), R)
        hi_ref[rows, :], lo_ref[rows, :] = split(v)

    def conv(ref, hi_ref, lo_ref, a, b):
        def body(s, _):
            put(hi_ref, lo_ref, s, ref[s])
            return 0
        lax.fori_loop(a, b, body, 0)

    scale = jnp.exp(jnp.full((1, 1), ls[0], F32))

    def logits(a, b, t0, t1):
        rows = slice(a * R, b * R)

        def body(t, _):
            cs = pl.ds(pl.multiple_of(t * 256, 256), 256)
            lg[rows, cs] = scale * dot3(ih[rows, :], il[rows, :], th[cs, :], tl[cs, :], ((1,), (1,)))
            return 0
        lax.fori_loop(t0, t1, body, 0)

    def ipass(h, p, q, primary, s):
        isend(h, p, q, primary, s, "A" if s == 1 else "B")

    def second(p):
        for h in (0, 1):
            iwait(h, p, 3)
            ipass(h, p, 3, False, 1)
            iwait(h, p, 1)
            ipass(h, p, 1, False, -1)

    def third(p):
        for h in (0, 1):
            iwait(h, p, 2)

    for h in (0, 1):
        isend(h, 0, 0, True, 1)
        isend(h, 0, 0, True, -1)
    for ch in (0, 1, 2):
        tsend(0, 1, ch)
        tsend(0, -1, ch)
    for h in (0, 1):
        isend(h, 0, 0, False, 1)
        isend(h, 0, 0, False, -1)
    tcore(0)
    put(ih, il, 0, img[0])
    put(th, tl, 0, txt[0])

    tpass(1, 0)
    for h in (0, 1):
        iwait(h, 3, 0)
        ipass(h, 3, 0, True, 1)
        iwait(h, 1, 0)
        ipass(h, 1, 0, True, -1)
    for p in (3, 1):
        for h in (0, 1):
            isend(h, p, 0, False, 1)
            isend(h, p, 0, False, -1)
    tpass(1, 1)
    second(0)
    tpass(1, 2)
    tcore(7)
    tcore(1)
    for h in (0, 1):
        iwait(h, 2, 0)
        isend(h, 2, 0, False, 1)
        isend(h, 2, 0, False, -1)
    conv(img, ih, il, 1, 5)
    tpass(2, 0)
    for dz in (0, 7, 1):
        cwait(dz)
    conv(txt, th, tl, 1, 6)
    tpass(2, 1)
    logits(0, 5, 0, 1)
    second(3)
    tpass(2, 2)
    tcore(6)
    tcore(2)
    second(1)
    tpass(3, 0)
    cwait(6)
    cwait(2)
    conv(img, ih, il, 5, 9)
    third(0)
    tpass(3, 1)
    conv(txt, th, tl, 6, 10)
    second(2)
    tpass(3, 2)
    tcore(5)
    tcore(3)
    conv(img, ih, il, 9, 11)
    logits(5, 11, 0, 1)
    third(3)
    cwait(5)
    cwait(3)
    conv(txt, th, tl, 10, 14)
    logits(0, 11, 1, 2)
    tlast()
    tcore(4)
    third(1)
    conv(img, ih, il, 11, 15)
    logits(11, 15, 0, 2)
    cwait(4)
    conv(txt, th, tl, 14, 16)
    logits(0, 15, 2, 3)
    third(2)
    conv(img, ih, il, 15, 16)
    logits(15, 16, 0, 3)

    RB = 2 * R
    NB = N // RB

    def rows_body(i, cm):
        rows = pl.ds(pl.multiple_of(i * RB, RB), RB)
        v = lg[rows, :]
        rm = jnp.max(v, axis=1, keepdims=True)
        e = jnp.exp(v - rm)
        er[rows, :] = e
        row_max[rows, :] = jnp.broadcast_to(rm, (RB, 128))
        rl = rm + jnp.log(jnp.sum(e, axis=1, keepdims=True))
        cols_a[rows, :] = jnp.broadcast_to(rl, (RB, 128))
        return jnp.maximum(cm, jnp.max(v.reshape(RB // 8, 8, N), axis=0))

    cm = lax.fori_loop(0, NB, rows_body, jnp.full((8, N), -jnp.inf, F32))
    cm = jnp.max(cm, axis=0, keepdims=True)

    def cols_body(i, cs):
        rows = pl.ds(pl.multiple_of(i * RB, RB), RB)
        e = jnp.exp(lg[rows, :] - cm)
        ec[rows, :] = e
        return cs + jnp.sum(e.reshape(RB // 8, 8, N), axis=0)

    NL = N // 128
    lane = lax.broadcasted_iota(jnp.int32, (128, 128), 1)

    def to_rows(ref):
        m = jnp.zeros((128, 128), F32)
        for b in range(NL):
            m = jnp.where(lane == b, ref[b * 128:(b + 1) * 128, :], m)
        return m.T[:8, :]

    def to_cols(ref, v):
        m = jnp.concatenate([v, jnp.zeros((120, 128), F32)], axis=0).T
        for b in range(NL):
            ref[b * 128:(b + 1) * 128, :] = jnp.broadcast_to(m[:, b:b + 1], (128, 128))

    def iabs(s):
        return ((x + IMG[s][0]) % 4) * 4 + (y + IMG[s][1]) % 4

    def tabs(s):
        return ((z + TXT[s][0]) % 8) * 2 + (k + TXT[s][1]) % 2

    def to_abs(where):
        for s in range(16):
            cols_b[pl.ds(pl.multiple_of(where(s) * R, R), R), :] = cols_a[s * R:(s + 1) * R, :]

    def to_rel(where):
        for s in range(16):
            cols_a[s * R:(s + 1) * R, :] = cols_b[pl.ds(pl.multiple_of(where(s) * R, R), R), :]

    me_p, me_r = x * 4 + y, z * 2 + k
    to_abs(iabs)
    rst[me_p] = to_rows(cols_b)
    plane = [send(rst.at[me_p], rst.at[me_p], o) for o in PLANE]
    cs = lax.fori_loop(0, NB, cols_body, jnp.zeros((8, N), F32))
    cl = cm + jnp.log(jnp.sum(cs, axis=0, keepdims=True))
    c8 = jnp.concatenate([cl[:, b * 128:(b + 1) * 128] for b in range(NL)] + [jnp.zeros((8 - NL, 128), F32)], axis=0)
    to_cols(cols_a, c8)
    to_abs(tabs)
    cst[me_r] = to_rows(cols_b)
    ring = [send(cst.at[me_r], cst.at[me_r], o) for o in RING]

    def merge(ref):
        v = ref[...]
        m = jnp.max(v, axis=0)
        return m + jnp.log(jnp.sum(jnp.exp(v - m[None]), axis=0))

    lane_n = lax.broadcasted_iota(jnp.int32, (1, N), 1)
    cid = lane_n
    for s, (dz, dk) in enumerate(TXT):
        base = shard_of(False, x, y, (z + dz) % 8, (k + dk) % 2) * R - s * R
        cid = jnp.where((lane_n >= s * R) & (lane_n < (s + 1) * R), lane_n + base, cid)

    sub = lax.broadcasted_iota(jnp.int32, (R, N), 0)

    def tile_rows(s):
        rows = pl.ds(pl.multiple_of(s * R, R), R)
        return rows, (cid - rid[s]) == sub

    def dots_body(s, c):
        rows, hit = tile_rows(s)
        v = lg[rows, :]
        a, d = c
        row_dot[rows, :] = jnp.broadcast_to(jnp.sum(er[rows, :] * v, axis=1, keepdims=True), (R, 128))
        a = a + jnp.sum((ec[rows, :] * v).reshape(R // 8, 8, N), axis=0)
        d = d + jnp.sum(jnp.where(hit, v, 0.0).reshape(R // 8, 8, N), axis=0)
        return a, d

    zero = jnp.zeros((8, N), F32)
    col_dot, diag = lax.fori_loop(0, 16, dots_body, (zero, zero))
    col_dot = jnp.sum(col_dot, axis=0, keepdims=True)
    diag = jnp.sum(diag)

    for c in plane:
        c.wait_recv()
    to_cols(cols_b, merge(rst))
    to_rel(iabs)
    row_sum = jnp.sum(cols_a[0:R, 0:1])
    row_max[...] = 0.5 * jnp.exp(row_max[...] - cols_a[...])
    for c in ring:
        c.wait_recv()
    to_cols(cols_b, merge(cst))
    to_rel(tabs)
    c8 = to_rows(cols_a)
    cl = jnp.concatenate([c8[b:b + 1, :] for b in range(NL)], axis=1)
    fc = 0.5 * jnp.exp(cm - cl)

    def weights_body(s, _):
        rows, hit = tile_rows(s)
        w = er[rows, :] * row_max[rows, 0:1] + ec[rows, :] * fc
        wh[rows, :], wl[rows, :] = split(jnp.where(hit, w - 1.0, w))
        return 0

    lax.fori_loop(0, 16, weights_body, 0)

    def transpose(b0, b1):
        def body(b, _):
            cs = pl.ds(pl.multiple_of(b * 128, 128), 128)
            wth[cs, :] = wh[:, cs].T
            wtl[cs, :] = wl[:, cs].T
            return 0
        lax.fori_loop(b0, b1, body, 0)

    def product(dst, ah, al, bh, bl, a, b):
        rows = slice(a * R, b * R)

        def body(n, _):
            cs = pl.ds(pl.multiple_of(n * (E // 2), 128), E // 2)
            dst[rows, cs] = dot3(ah[rows, :], al[rows, :], bh[:, cs], bl[:, cs], ((1,), (0,)))
            return 0
        lax.fori_loop(0, 2, body, 0)

    def image_product(a, b):
        product(gi, wh, wl, th, tl, a, b)

    def text_product(a, b):
        product(gt, wth, wtl, ih, il, a, b)

    COL = {"f": slice(0, E), "A": slice(0, EH), "B": slice(EH, E)}
    red = {}

    def grows(h, o):
        return ISLOT[o] * R + h * H

    def quarter(h, p):
        o = pos(h, p, 2)
        r = pl.ds(grows(h, o), H)
        red[("q", h, p, 1)] = send(gi.at[r, HALF["A"]], rq.at[h, p, 0], idir(h, False, 1))
        red[("q", h, p, 3)] = send(gi.at[r, HALF["B"]], rq.at[h, p, 1], idir(h, False, -1))

    def unit(h, p):
        for q, part, j, s in ((1, "A", 0, 1), (3, "B", 1, -1)):
            red.pop(("q", h, p, q)).wait_recv()
            a = grows(h, pos(h, p, q))
            gi[a:a + H, COL[part]] += rq[h, p, j]
            red[("u", h, p, q)] = send(gi.at[pl.ds(a, H), :], ru.at[h, p, j], idir(h, False, s))

    def gathered(h, p):
        a = grows(h, pos(h, p, 0))
        for q in (1, 3):
            red.pop(("u", h, p, q)).wait_recv()
        gi[a:a + H, :] += ru[h, p, 0] + ru[h, p, 1]

    def pquarter(h):
        r = pl.ds(grows(h, pos(h, 2, 0)), H)
        red[("pq", h, 1)] = send(gi.at[r, HALF["A"]], rpq.at[h, 0], idir(h, True, 1))
        red[("pq", h, 3)] = send(gi.at[r, HALF["B"]], rpq.at[h, 1], idir(h, True, -1))

    def punit(h):
        for p, part, j, s in ((1, "A", 0, 1), (3, "B", 1, -1)):
            red.pop(("pq", h, p)).wait_recv()
            a = grows(h, pos(h, p, 0))
            gi[a:a + H, COL[part]] += rpq[h, j]
            red[("pu", h, p)] = send(gi.at[pl.ds(a, H), :], rpu.at[h, j], idir(h, True, s))

    def image_out(h):
        for p in (1, 3):
            red.pop(("pu", h, p)).wait_recv()
        a = grows(h, (0, 0))
        out_i[h * H:(h + 1) * H, :] = scale * (gi[a:a + H, :] + (rpu[h, 0] + rpu[h, 1]))

    def core_send(dz):
        red[("c", dz)] = send(gt.at[pl.ds(TSLOT[(dz, 1)] * R, R), :], rc.at[dz], CORE)

    def core_add(dz):
        red.pop(("c", dz)).wait_recv()
        a = TSLOT[(dz, 0)] * R
        gt[a:a + R, :] += rc[dz]

    def zsend(dz, s, ch):
        a, n = CHUNK[ch]
        src = gt.at[pl.ds(TSLOT[(dz, 0)] * R + a, n), :]
        red[("z", (dz - s) % 8, s, ch)] = send(src, rz.at[dz, pl.ds(a, n), :], zdir(s))

    def zadd(dz, s, ch):
        red.pop(("z", dz, s, ch)).wait_recv()
        a, n = CHUNK[ch]
        g = TSLOT[(dz, 0)] * R + a
        gt[g:g + n, :] += rz[(dz + s) % 8, a:a + n, :]

    def zstep(d, j):
        for dz, s, ch in ((d, 1, (2, 0, 1)[j]), (8 - d, -1, (0, 2, 1)[j])):
            if d == 3:
                came = None if j == 0 else ch if j == 1 else ("p" if s == 1 else "m")
            else:
                came = ch
            if came is not None:
                zadd(dz % 8, s, came)
            if d > 0:
                zsend(dz, s, ch)

    transpose(NL - 1, NL)
    text_product(14, 16)
    core_send(4)
    image_product(11, 16)
    for p in (2, 3, 1):
        for h in (0, 1):
            quarter(h, p)
    core_add(4)
    for s, ch in ((1, 0), (-1, 2), (1, "p"), (-1, "m")):
        zsend(4, s, ch)
    transpose(NL // 2, NL - 1)
    text_product(10, 14)
    for dz in (3, 5):
        core_send(dz)
    for h in (0, 1):
        unit(h, 2)
    for dz in (3, 5):
        core_add(dz)
    zstep(3, 0)
    image_product(5, 11)
    for h in (0, 1):
        quarter(h, 0)
    zstep(3, 1)
    for p in (3, 1):
        for h in (0, 1):
            unit(h, p)
    zstep(3, 2)

    scale_part = (jnp.sum(row_max[:, 0:1] * row_dot[:, 0:1]) + jnp.sum(fc * col_dot) - diag) / batch
    col_sum = jnp.sum(jnp.where(lane_n < R, cl, 0.0))
    loss_part = (row_sum + col_sum - 2.0 * diag) / (2.0 * batch)
    sub8 = lax.broadcasted_iota(jnp.int32, (8, 128), 0)
    pst[me_p] = jnp.where(sub8 == 0, loss_part, jnp.where(sub8 == 1, scale_part, 0.0))
    plane = [send(pst.at[me_p], pst.at[me_p], o) for o in PLANE]

    transpose(0, NL // 2)
    text_product(6, 10)
    for dz in (2, 6):
        core_send(dz)
    image_product(0, 5)
    for dz in (2, 6):
        core_add(dz)
    zstep(2, 0)
    zstep(2, 1)
    for h in (0, 1):
        gathered(h, 2)
        pquarter(h)
    zstep(2, 2)
    for h in (0, 1):
        unit(h, 0)
    text_product(0, 6)
    for dz in (1, 7, 0):
        core_send(dz)
    for c in plane:
        c.wait_recv()
    zst[me_r] = jnp.sum(pst[...], axis=0)
    ring = [send(zst.at[me_r], zst.at[me_r], o) for o in RING]
    for dz in (1, 7, 0):
        core_add(dz)
    zstep(1, 0)
    zstep(1, 1)
    for h in (0, 1):
        gathered(h, 3)
        gathered(h, 1)
        punit(h)
    zstep(1, 2)
    for c in ring:
        c.wait_recv()
    out_s[...] = jnp.sum(zst[...], axis=0)
    for h in (0, 1):
        gathered(h, 0)
    for j in (0, 1, 2):
        zstep(0, j)
    out_t[...] = scale * gt[0:R, :]
    for h in (0, 1):
        image_out(h)
    for c in copies:
        c.wait_send()


def finish(gi, gt, s, out_i, out_t, out_loss, out_scale):
    out_i[...] = gi[...]
    out_t[...] = gt[...]
    out_loss[0] = jnp.max(s[0:1, 0:1])
    out_scale[0] = jnp.max(s[1:2, 0:1])


def per_device(image, text, log_scale):
    R, E = image.shape
    N = 16 * R
    batch = 256 * R
    H, EH = R // 2, E // 2
    vm = pltpu.VMEM
    vspec = pl.BlockSpec(memory_space=pltpu.VMEM)
    sspec = pl.BlockSpec(memory_space=pltpu.SMEM)
    hspec = pl.BlockSpec(memory_space=pltpu.HBM)
    one = jax.ShapeDtypeStruct((1,), F32)
    grad = jax.ShapeDtypeStruct((R, E), F32)
    gi, gt, s = pl.pallas_call(
        functools.partial(kernel, R, E, float(batch)),
        out_shape=(grad, grad, jax.ShapeDtypeStruct((8, 128), F32)),
        in_specs=[hspec, hspec, hspec],
        out_specs=(vspec, vspec, vspec),
        scratch_shapes=[
            vm((16, R, E), F32), vm((16, R, E), F32),
            vm((N, E), BF16), vm((N, E), BF16), vm((N, E), BF16), vm((N, E), BF16),
            vm((N, N), F32), vm((N, N), F32), vm((N, N), F32), vm((N, N), BF16), vm((N, N), BF16), vm((N, N), BF16), vm((N, N), BF16),
            vm((N, E), F32), vm((N, E), F32),
            vm((2, 4, 2, H, EH), F32), vm((2, 4, 2, H, E), F32),
            vm((2, 2, H, EH), F32), vm((2, 2, H, E), F32),
            vm((8, R, E), F32), vm((8, R, E), F32),
            vm((N, 128), F32), vm((N, 128), F32), vm((N, 128), F32), vm((N, 128), F32),
            vm((16, 8, 128), F32), vm((16, 8, 128), F32), vm((16, 8, 128), F32), vm((16, 8, 128), F32),
            pltpu.SMEM((1,), F32), pltpu.SMEM((16,), jnp.int32), pltpu.SemaphoreType.DMA((3,)),
            pltpu.SemaphoreType.DMA((N_COPIES,)), pltpu.SemaphoreType.DMA((N_COPIES,)),
        ],
        compiler_params=pltpu.CompilerParams(collective_id=0, has_side_effects=True, vmem_limit_bytes=54 * 2**20),
        cost_estimate=pl.CostEstimate(flops=18 * N * N * E, bytes_accessed=16 * R * E, transcendentals=6 * N * N),
    )(image, text, log_scale)
    out_i, out_t, loss, scale_grad = pl.pallas_call(
        finish,
        out_shape=(grad, grad, one, one),
        in_specs=[vspec, vspec, vspec],
        out_specs=(vspec, vspec, sspec, sspec),
    )(gi, gt, s)
    return loss, out_i, out_t, scale_grad


def solution(mesh):
    return jax.shard_map(
        per_device,
        mesh=mesh,
        in_specs=(P(("row", "col"), None), P(("col", "row"), None), P()),
        out_specs=(P(), P(("row", "col"), None), P(("col", "row"), None), P()),
        check_vma=False,
    )
```

time: 94.2 us -> 85.5 us (0.908)
  between operations: 4.81 us -> 1.29 us
  Pallas kernels: 86.8 us -> 83.9 us
  local copies, waits for them, and re-layouts: 2.39 us -> 0 us
    pallas_call x1, Pallas kernels: 86.8 us -> 82 us  [per_device(): pl.pallas_call(functools.partial(kernel, R, E, float(batch)), out_shape=(...]
    unnamed x4 -> x0, local copies, waits for them, and re-layouts: 2.39 us -> none
    pallas_call x0 -> x1, Pallas kernels: none -> 1.87 us  [per_device(): pl.pallas_call(finish, out_shape=(grad, grad, one, one), in_specs=[vspec,...]
where the time goes in v2:
time: 85.5 us; the launch traced here: 85.2 us
  Pallas kernels  83.9 us (98%)
  between operations  1.29 us (2%)
    pallas_call x1, Pallas kernels, per_device(): pl.pallas_call(functools.partial(kernel, R, E, float(batch)), out_shape=(...  82 us
    pallas_call x1, Pallas kernels, per_device(): pl.pallas_call(finish, out_shape=(grad, grad, one, one), in_specs=[vspec,...  1.87 us

profile of v2, /device:TPU:1, one launch (start us, length us, event | category | flops | bytes accessed | tf_op | source)
XLA Modules:
  0.0 85.2 jit_solution(14634011997132427627)
XLA Ops:
  1.3 82.0 %shard_map.66 = (f32[48,1280]{1,0:T(8,128)}, f32[48,1280]{1,0:T(8,128)}, f32[8,128]{1,0:T(8,128)}) custom-call(f32[48,1280]{1,0:T(8,128)} %im.1, f32[48,1280]{1,0:T(8,128)} %tx.1, f32[1]{0:T(128)S(6)} %copy.7.ls_hbm), custom_call_target="tpu_custom_call" | custom-call | flops 13589544960 | bytes 983040 | tf_op jit(solution)/shard_map/pallas_call | solution.py:553
  83.3 1.9 %shard_map.67 = (f32[48,1280]{1,0:T(8,128)}, f32[48,1280]{1,0:T(8,128)}, f32[1]{0:T(128)}, f32[1]{0:T(128)}) custom-call(f32[48,1280]{1,0:T(8,128)} %get-tuple-element.11.gi, f32[48,1280]{1,0:T(8,128)} %get-tuple-element.12.gt, f32[8,128]{1,0:T(8,128)} %get-tuple-element.13.s), custom_call_target="tpu_custom_call" | custom-call | tf_op jit(solution)/shard_map/pallas_call | solution.py:574

commit v3 on v2

--- a/solution.py
+++ b/solution.py
@@ -20,6 +20,7 @@
 TSLOT = {p: i for i, p in enumerate(TXT)}
 PLANE = [(x, y, 0, 0) for x in (2, 3, 1, 0) for y in (2, 3, 1, 0) if (x, y) != (0, 0)]
 RING = [(0, 0, z, k) for z in (4, 3, 5, 2, 6, 1, 7, 0) for k in (1, 0) if (z, k) != (0, 0)]
+NEXT = [(1, 0, 0, 0), (3, 0, 0, 0), (0, 1, 0, 0), (0, 3, 0, 0), (0, 0, 1, 0), (0, 0, 7, 0), (0, 0, 0, 1)]
 N_COPIES = 208
 CHUNK = {0: (0, 16), 1: (16, 16), 2: (32, 16), "p": (16, 8), "m": (24, 8)}
 
@@ -81,7 +82,7 @@
     HALF = {"f": pl.ds(0, E), "A": pl.ds(0, EH), "B": pl.ds(EH, EH)}
 
     barrier = pltpu.get_barrier_semaphore()
-    for o in PLANE + RING:
+    for o in NEXT:
         pl.semaphore_signal(barrier, inc=1, device_id=peer(o), device_id_type=MESH)
     local = [pltpu.make_async_copy(im, img.at[0], lsem.at[0]), pltpu.make_async_copy(tx, txt.at[0], lsem.at[1]),
              pltpu.make_async_copy(ls_hbm, ls, lsem.at[2])]
@@ -91,7 +92,7 @@
         rid[s] = shard_of(True, (x + dx) % 4, (y + dy) % 4, z, k) * R
     for c in local:
         c.wait()
-    pl.semaphore_wait(barrier, len(PLANE) + len(RING))
+    pl.semaphore_wait(barrier, len(NEXT))
 
     got = {}
 
@@ -124,6 +125,16 @@
     def tlast():
         for ch in (0, "p", "m", 2):
             got.pop(("t", 4, ch)).wait_recv()
+
+    def tlast_core():
+        for ch in (0, 2, "p", "m"):
+            got.pop(("t", 4, ch)).wait_recv()
+            rows = pl.ds(*CHUNK[ch])
+            got[("c4", ch)] = send(txt.at[TSLOT[(4, 0)], rows, :], txt.at[TSLOT[(4, 1)], rows, :], CORE)
+
+    def cwait4():
+        for ch in (0, 2, "p", "m"):
+            got.pop(("c4", ch)).wait_recv()
 
     def tcore(dz):
         got[("c", dz)] = send(txt.at[TSLOT[(dz, 0)]], txt.at[TSLOT[(dz, 1)]], CORE)
@@ -228,12 +239,11 @@
     cwait(3)
     conv(txt, th, tl, 10, 14)
     logits(0, 11, 1, 2)
-    tlast()
-    tcore(4)
+    tlast_core()
     third(1)
     conv(img, ih, il, 11, 15)
     logits(11, 15, 0, 2)
-    cwait(4)
+    cwait4()
     conv(txt, th, tl, 14, 16)
     logits(0, 15, 2, 3)
     third(2)

time: 85.5 us -> 84.1 us (0.984)
  Pallas kernels: 83.9 us -> 82.7 us
    pallas_call x1, Pallas kernels: 82 us -> 80.9 us  [per_device(): pl.pallas_call(functools.partial(kernel, R, E, float(batch)), out_shape=(...]
where the time goes in v3:
time: 84.1 us; the launch traced here: 84 us
  Pallas kernels  82.7 us (98%)
  between operations  1.29 us (2%)
    pallas_call x1, Pallas kernels, per_device(): pl.pallas_call(functools.partial(kernel, R, E, float(batch)), out_shape=(...  80.9 us
    pallas_call x1, Pallas kernels, per_device(): pl.pallas_call(finish, out_shape=(grad, grad, one, one), in_specs=[vspec,...  1.87 us

profile of v3, /device:TPU:1, one launch (start us, length us, event | category | flops | bytes accessed | tf_op | source)
XLA Modules:
  0.0 84.0 jit_solution(16952840431334862195)
XLA Ops:
  1.3 80.9 %shard_map.66 = (f32[48,1280]{1,0:T(8,128)}, f32[48,1280]{1,0:T(8,128)}, f32[8,128]{1,0:T(8,128)}) custom-call(f32[48,1280]{1,0:T(8,128)} %im.1, f32[48,1280]{1,0:T(8,128)} %tx.1, f32[1]{0:T(128)S(6)} %copy.7.ls_hbm), custom_call_target="tpu_custom_call" | custom-call | flops 13589544960 | bytes 983040 | tf_op jit(solution)/shard_map/pallas_call | solution.py:563
  82.1 1.9 %shard_map.67 = (f32[48,1280]{1,0:T(8,128)}, f32[48,1280]{1,0:T(8,128)}, f32[1]{0:T(128)}, f32[1]{0:T(128)}) custom-call(f32[48,1280]{1,0:T(8,128)} %get-tuple-element.11.gi, f32[48,1280]{1,0:T(8,128)} %get-tuple-element.12.gt, f32[8,128]{1,0:T(8,128)} %get-tuple-element.13.s), custom_call_target="tpu_custom_call" | custom-call | tf_op jit(solution)/shard_map/pallas_call | solution.py:584

commit v4 on v3

--- a/solution.py
+++ b/solution.py
@@ -42,7 +42,9 @@
 
 def dot3(ah, al, bh, bl, dims):
     d = functools.partial(lax.dot_general, dimension_numbers=(dims, ((), ())), preferred_element_type=F32)
-    return d(ah, bh) + (d(al, bh) + d(ah, bl))
+    m = ah.shape[0]
+    t = d(jnp.concatenate([ah, al], axis=0), bh)
+    return t[:m] + (t[m:] + d(ah, bl))
 
 
 def kernel(R, E, batch, im, tx, ls_hbm, out_i, out_t, out_s,
@@ -478,10 +480,10 @@
         core_send(dz)
     for h in (0, 1):
         unit(h, 2)
+    image_product(5, 11)
     for dz in (3, 5):
         core_add(dz)
     zstep(3, 0)
-    image_product(5, 11)
     for h in (0, 1):
         quarter(h, 0)
     zstep(3, 1)

time: 84.1 us -> 83 us (0.987)
  Pallas kernels: 82.7 us -> 81.6 us
    pallas_call x1, Pallas kernels: 80.9 us -> 79.7 us  [per_device(): pl.pallas_call(functools.partial(kernel, R, E, float(batch)), out_shape=(...]
where the time goes in v4:
time: 83 us; the launch traced here: 82.9 us
  Pallas kernels  81.6 us (98%)
  between operations  1.29 us (2%)
    pallas_call x1, Pallas kernels, per_device(): pl.pallas_call(functools.partial(kernel, R, E, float(batch)), out_shape=(...  79.7 us
    pallas_call x1, Pallas kernels, per_device(): pl.pallas_call(finish, out_shape=(grad, grad, one, one), in_specs=[vspec,...  1.87 us

profile of v4, /device:TPU:1, one launch (start us, length us, event | category | flops | bytes accessed | tf_op | source)
XLA Modules:
  0.0 82.9 jit_solution(8775923794351651977)
XLA Ops:
  1.3 79.7 %shard_map.66 = (f32[48,1280]{1,0:T(8,128)}, f32[48,1280]{1,0:T(8,128)}, f32[8,128]{1,0:T(8,128)}) custom-call(f32[48,1280]{1,0:T(8,128)} %im.1, f32[48,1280]{1,0:T(8,128)} %tx.1, f32[1]{0:T(128)S(6)} %copy.7.ls_hbm), custom_call_target="tpu_custom_call" | custom-call | flops 13589544960 | bytes 983040 | tf_op jit(solution)/shard_map/pallas_call | solution.py:565
  81.0 1.9 %shard_map.67 = (f32[48,1280]{1,0:T(8,128)}, f32[48,1280]{1,0:T(8,128)}, f32[1]{0:T(128)}, f32[1]{0:T(128)}) custom-call(f32[48,1280]{1,0:T(8,128)} %get-tuple-element.11.gi, f32[48,1280]{1,0:T(8,128)} %get-tuple-element.12.gt, f32[8,128]{1,0:T(8,128)} %get-tuple-element.13.s), custom_call_target="tpu_custom_call" | custom-call | tf_op jit(solution)/shard_map/pallas_call | solution.py:586

commit v5 on v4

--- a/solution.py
+++ b/solution.py
@@ -492,6 +492,11 @@
             unit(h, p)
     zstep(3, 2)
 
+    transpose(0, NL // 2)
+    text_product(6, 10)
+    for dz in (2, 6):
+        core_send(dz)
+
     scale_part = (jnp.sum(row_max[:, 0:1] * row_dot[:, 0:1]) + jnp.sum(fc * col_dot) - diag) / batch
     col_sum = jnp.sum(jnp.where(lane_n < R, cl, 0.0))
     loss_part = (row_sum + col_sum - 2.0 * diag) / (2.0 * batch)
@@ -499,10 +504,6 @@
     pst[me_p] = jnp.where(sub8 == 0, loss_part, jnp.where(sub8 == 1, scale_part, 0.0))
     plane = [send(pst.at[me_p], pst.at[me_p], o) for o in PLANE]
 
-    transpose(0, NL // 2)
-    text_product(6, 10)
-    for dz in (2, 6):
-        core_send(dz)
     image_product(0, 5)
     for dz in (2, 6):
         core_add(dz)

time: 83 us -> 82.8 us (level)
  no operation moved by 1% of the time
where the time goes in v5:
time: 82.8 us; the launch traced here: 82.7 us
  Pallas kernels  81.4 us (98%)
  between operations  1.29 us (2%)
    pallas_call x1, Pallas kernels, per_device(): pl.pallas_call(functools.partial(kernel, R, E, float(batch)), out_shape=(...  79.5 us
    pallas_call x1, Pallas kernels, per_device(): pl.pallas_call(finish, out_shape=(grad, grad, one, one), in_specs=[vspec,...  1.87 us

profile of v5, /device:TPU:1, one launch (start us, length us, event | category | flops | bytes accessed | tf_op | source)
XLA Modules:
  0.0 82.7 jit_solution(1600599518594867673)
XLA Ops:
  1.3 79.5 %shard_map.66 = (f32[48,1280]{1,0:T(8,128)}, f32[48,1280]{1,0:T(8,128)}, f32[8,128]{1,0:T(8,128)}) custom-call(f32[48,1280]{1,0:T(8,128)} %im.1, f32[48,1280]{1,0:T(8,128)} %tx.1, f32[1]{0:T(128)S(6)} %copy.7.ls_hbm), custom_call_target="tpu_custom_call" | custom-call | flops 13589544960 | bytes 983040 | tf_op jit(solution)/shard_map/pallas_call | solution.py:566
  80.8 1.9 %shard_map.67 = (f32[48,1280]{1,0:T(8,128)}, f32[48,1280]{1,0:T(8,128)}, f32[1]{0:T(128)}, f32[1]{0:T(128)}) custom-call(f32[48,1280]{1,0:T(8,128)} %get-tuple-element.11.gi, f32[48,1280]{1,0:T(8,128)} %get-tuple-element.12.gt, f32[8,128]{1,0:T(8,128)} %get-tuple-element.13.s), custom_call_target="tpu_custom_call" | custom-call | tf_op jit(solution)/shard_map/pallas_call | solution.py:587
